TPU v7x, 32 devices: a whole 2x2x4 slice. The times are simulated.
32 devices in a mesh: win: 4 (over x, core), srow: 4 (over z), scol: 2 (over y).
Axes of the slice: x: 2, y: 2, z: 4, core: 2. Of those that a mesh axis runs over, the one named last changes fastest.
Arguments:
- spectra: float32 [4, 2, 64, 4096], P(None, None, 'win', ('srow', 'scol')), may hold values from -6 to 6
- bins: int32 [4], replicated, may hold values from 1 to 2047
- travel: int32 [4096, 2048], P(('srow', 'scol'), 'win'), may hold values from 0 to 16383
Outputs:
- coherence: bfloat16 [4, 2, 4096, 4, 1024], P('win', None, 'srow', None, 'scol')
- beam: float32 [4, 2048], P('win')
All inputs are finite; a program needn't handle non-finite values.
Results may differ from a plain program's by a relative error of at most 0.012.
Values may be sent and summed in bfloat16 or wider, within the bound.
A program may use at most 128 MiB of HBM per device.

v0:
```python
import functools
import math

import jax
import jax.numpy as jnp
import numpy as np
from jax import lax
from jax.experimental import pallas as pl
from jax.experimental.pallas import tpu as pltpu
from jax.sharding import PartitionSpec as P

NFFT = 4096
MESH = pl.DeviceIdType.MESH
MAGIC = 12582912.0
ROWS = 256


def phase_normalized(spectra):
    magnitude = jnp.sqrt(spectra[:, 0] * spectra[:, 0] + spectra[:, 1] * spectra[:, 1] + 0.5)
    return (spectra / magnitude[:, None]).astype(jnp.bfloat16)


def fitted():
    nodes = 0.25 * (1.0 - np.cos(np.pi * (np.arange(64) + 0.5) / 64)) / 2.0
    root = np.sqrt(nodes)
    powers = np.vander(nodes, 5, increasing=True)
    sine = np.linalg.lstsq(powers, np.sin(np.pi * root) / root, rcond=None)[0]
    cosine = np.linalg.lstsq(powers, -2.0 * np.cos(np.pi * root), rcond=None)[0]
    return [float(a) for a in sine], [float(a) for a in cosine]


def steer(travel, scale):
    sine, cosine = fitted()
    turns = travel.astype(jnp.int32).astype(jnp.float32) * scale
    rest = turns - ((turns + MAGIC) - MAGIC)
    z = rest * rest
    s = sine[4]
    c = cosine[4]
    for k in (3, 2, 1, 0):
        s = s * z + sine[k]
        c = c * z + cosine[k]
    s = s * rest
    return 1.0 - 2.0 * (s * s), s * c


def exchange_kernel(nw, nr, nc, x_ref, t_ref, xg, tcol, trow, xloc, send, recv, local):
    w, r, c = lax.axis_index("win"), lax.axis_index("srow"), lax.axis_index("scol")
    core = lax.rem(w, 2)
    mate = {"win": w + 1 - 2 * core}
    number = {}

    def slot(*name):
        return number.setdefault(name, len(number))

    def make(name, src, dst, where):
        k = slot(*name)
        return pltpu.make_async_remote_copy(
            src_ref=src, dst_ref=dst, send_sem=send.at[k], recv_sem=recv.at[k],
            device_id=where, device_id_type=MESH,
        )

    pending = []

    def start(cond, name, src, dst, where):
        copy = make(name, src, dst, where)
        if cond is True:
            copy.start()
        else:
            pl.when(cond)(copy.start)
        pending.append((cond, copy))

    def arrived(cond, name, dst):
        copy = make(name, dst, dst, mate)
        if cond is True:
            copy.wait_recv()
        else:
            pl.when(cond)(copy.wait_recv)

    barrier = pltpu.get_barrier_semaphore()

    def greet(where):
        pl.semaphore_signal(barrier, inc=1, device_id=where, device_id_type=MESH)

    pl.when(r > 0)(lambda: greet({"srow": r - 1}))
    pl.when(r < nr - 1)(lambda: greet({"srow": r + 1}))
    for d in range(1, nc):
        greet({"scol": lax.rem(c + d, nc)})
    for d in range(1, nw):
        greet({"win": lax.rem(w + d, nw)})
    ends = jnp.where(r > 0, 1, 0) + jnp.where(r < nr - 1, 1, 0)
    pl.semaphore_wait(barrier, ends + nc - 1 + nw - 1)

    locals_t = [
        pltpu.make_async_copy(t_ref.at[0], tcol.at[core, 0, 0], local.at[0]),
        pltpu.make_async_copy(t_ref.at[1], tcol.at[core, 1, 0], local.at[1]),
        pltpu.make_async_copy(t_ref, trow.at[core, c], local.at[2]),
    ]

    def chain_x(s):
        start((r < nr - 1) & (r >= s), ("xu", s + 1),
              x_ref if s == 0 else xloc.at[jnp.maximum(r - s, 0)],
              xloc.at[jnp.maximum(r - s, 0)], {"srow": r + 1})
        start((r > 0) & (r + s < nr), ("xd", s + 1),
              x_ref if s == 0 else xloc.at[jnp.minimum(r + s, nr - 1)],
              xloc.at[jnp.minimum(r + s, nr - 1)], {"srow": r - 1})

    def chain_t(s):
        start((r < nr - 1) & (r >= s), ("tu", s + 1),
              t_ref.at[0] if s == 0 else tcol.at[core, 0, s],
              tcol.at[core, 0, s + 1], {"srow": r + 1})
        start((r > 0) & (r + s < nr), ("td", s + 1),
              t_ref.at[1] if s == 0 else tcol.at[core, 1, s],
              tcol.at[core, 1, s + 1], {"srow": r - 1})

    chain_x(0)
    for d in range(1, nc):
        start(True, ("xc", d), x_ref, xloc.at[nr + c], {"scol": lax.rem(c + d, nc)})
    chain_t(0)
    for d in range(1, nc):
        start(True, ("tc", d), t_ref, trow.at[core, c], {"scol": lax.rem(c + d, nc)})
    for copy in locals_t:
        copy.start()
    xloc[r] = x_ref[...]
    xloc[nr + c] = x_ref[...]
    for h in range(2):
        start(True, ("p", h, 0), t_ref.at[h], tcol.at[core, h, 0], mate)
    for s in range(1, nr):
        arrived(r >= s, ("xu", s), xloc.at[jnp.maximum(r - s, 0)])
        arrived(r + s < nr, ("xd", s), xloc.at[jnp.minimum(r + s, nr - 1)])
        if s < nr - 1:
            chain_x(s)
    for d in range(1, nc):
        arrived(True, ("xc", d), xloc.at[nr + lax.rem(c + nc - d, nc)])
    for d in range(1, nw):
        to = lax.rem(w + d, nw)
        start(True, ("xw", d), xloc.at[:, lax.rem(to, 2)], xg.at[w], {"win": to})
    own = pltpu.make_async_copy(xloc.at[:, core], xg.at[w], local.at[3])
    own.start()
    for d in range(1, nc):
        arrived(True, ("tc", d), trow.at[core, lax.rem(c + nc - d, nc)])
    for copy in locals_t:
        copy.wait()
    start(True, ("pr",), trow.at[core], trow.at[core], mate)
    for s in range(1, nr):
        arrived(r >= s, ("tu", s), tcol.at[core, 0, s])
        arrived(r + s < nr, ("td", s), tcol.at[core, 1, s])
        if s < nr - 1:
            chain_t(s)
        start(r >= s, ("p", 0, s), tcol.at[core, 0, s], tcol.at[core, 0, s], mate)
        start(r + s < nr, ("p", 1, s), tcol.at[core, 1, s], tcol.at[core, 1, s], mate)
    for d in range(1, nw):
        arrived(True, ("xw", d), xg.at[lax.rem(w + nw - d, nw)])
    own.wait()
    arrived(True, ("pr",), trow.at[1 - core])
    for s in range(nr):
        arrived(True if s == 0 else r >= s, ("p", 0, s), tcol.at[1 - core, 0, s])
        arrived(True if s == 0 else r + s < nr, ("p", 1, s), tcol.at[1 - core, 1, s])
    for cond, copy in pending:
        if cond is True:
            copy.wait_send()
        else:
            pl.when(cond)(copy.wait_send)


def exchange(x, t, nw, nr, nc):
    half_f, wl, n = x.shape[1], x.shape[3], x.shape[4]
    ph = t.shape[2]
    count = 4 * nr + 2 * nc + nw + 2 * nr + 2
    anywhere = pl.BlockSpec(memory_space=pl.ANY)
    return pl.pallas_call(
        functools.partial(exchange_kernel, nw, nr, nc),
        out_shape=(
            jax.ShapeDtypeStruct((nw, nr + nc, half_f, 2, wl, n), x.dtype),
            jax.ShapeDtypeStruct((2, 2, nr, n, ph), t.dtype),
            jax.ShapeDtypeStruct((2, nc, 2, n, ph), t.dtype),
        ),
        in_specs=[pl.BlockSpec(memory_space=pltpu.VMEM)] * 2,
        out_specs=(anywhere,) * 3,
        scratch_shapes=[
            pltpu.VMEM((nr + nc, 2, half_f, 2, wl, n), x.dtype),
            pltpu.SemaphoreType.DMA((count,)),
            pltpu.SemaphoreType.DMA((count,)),
            pltpu.SemaphoreType.DMA((4,)),
        ],
        compiler_params=pltpu.CompilerParams(collective_id=0, has_side_effects=True),
        name="exchange",
    )(x, t)


def beam_kernel(nr, nc, total, info, xrow, xcr, xci, tcol, trow, coh, part, kscr, csteer, rsteer):
    fi, t = pl.program_id(0), pl.program_id(1)
    r = info[0]
    scale = info[2 + fi].astype(jnp.float32) * (1.0 / NFFT)
    rows = xrow.shape[1]
    n, ph = tcol.shape[3], tcol.shape[4]
    step = 32

    @pl.when((fi == 0) & (t == 0))
    def _():
        part[...] = jnp.zeros_like(part)

    for slab in range(2):
        @pl.loop(0, n // step)
        def _(i):
            at = pl.ds(pl.multiple_of(i * step, step), step)
            cr, ci = steer(tcol[slab, 0, 0, at, :], scale)
            cr, ci = cr.astype(jnp.bfloat16), ci.astype(jnp.bfloat16)
            csteer[0, slab, at, :] = cr
            csteer[1, slab, at, :] = ci
            csteer[2, slab, at, :] = cr + ci

    @pl.when((t == 0) | (t == r + 1))
    def _():
        for slab in range(2):
            for block in range(nc):
                @pl.loop(0, n // step)
                def _(i):
                    at = pl.ds(pl.multiple_of(i * step, step), step)
                    to = pl.ds(pl.multiple_of(block * n + i * step, step), step)
                    rr, ri = steer(trow[slab, block, 0, at, :], scale)
                    rsteer[0, slab, to, :] = rr.astype(jnp.bfloat16).astype(jnp.float32)
                    rsteer[1, slab, to, :] = ri.astype(jnp.bfloat16).astype(jnp.float32)

    chunk = min(ROWS, rows)

    @pl.when(t != r + 1)
    def _():
        @pl.loop(0, rows // chunk)
        def _(m):
            at = pl.ds(pl.multiple_of(m * chunk, chunk), chunk)
            left = xrow[0, at, :]
            re = jnp.dot(left, xcr[0, 0], preferred_element_type=jnp.float32)
            im = jnp.dot(left, xci[0, 0], preferred_element_type=jnp.float32)
            inverse = lax.rsqrt(re * re + im * im + float(total))
            kr = (re * inverse).astype(jnp.bfloat16)
            ki = (im * inverse).astype(jnp.bfloat16)
            kscr[0, at, :] = kr
            kscr[1, at, :] = ki
            kscr[2, at, :] = kr + ki

            @pl.when(fi == 0)
            def _():
                coh[0, at, :] = kr
                coh[1, at, :] = ki

    half = jnp.where(t <= r, 0, 1)
    weight = jnp.where((t == r) | (t == r + 1), 1.0, 2.0)

    @pl.loop(0, rows // chunk)
    def _(m):
        at = pl.ds(pl.multiple_of(m * chunk, chunk), chunk)
        for slab in range(2):
            t1 = jnp.dot(kscr[0, at, :], csteer[0, slab], preferred_element_type=jnp.float32)
            t2 = jnp.dot(kscr[1, at, :], csteer[1, slab], preferred_element_type=jnp.float32)
            t3 = jnp.dot(kscr[2, at, :], csteer[2, slab], preferred_element_type=jnp.float32)
            v = rsteer[0, slab, at, :] * (t1 - t2) + rsteer[1, slab, at, :] * (t3 - (t1 + t2))
            v = jnp.sum(v.reshape(chunk // 8, 8, ph), axis=0)
            part[fi, half, slab] += weight * v


def beam_call(info, xrow, xcr, xci, tcol, trow, total):
    half_f, rows, depth = xrow.shape
    nr, n = xcr.shape[1], xcr.shape[3]
    nc, ph = trow.shape[1], trow.shape[4]

    def freq(fi, info):
        return lax.rem(info[1] + fi, half_f)

    def plane(t, info):
        return jnp.where(t <= info[0], t, t - 1)

    def col_map(fi, t, info):
        return (freq(fi, info), plane(t, info), 0, 0)

    def tcol_map(fi, t, info):
        r = info[0]
        return (0, jnp.where(t <= r, 0, 1), jnp.where(t <= r, r - t, t - 1 - r), 0, 0)

    def coh_map(fi, t, info):
        return (0, 0, jnp.where(fi == 0, plane(t, info), nr - 1))

    return pl.pallas_call(
        functools.partial(beam_kernel, nr, nc, total),
        out_shape=(
            jax.ShapeDtypeStruct((2, rows, nr * n), jnp.bfloat16),
            jax.ShapeDtypeStruct((half_f, 2, 2, 8, ph), jnp.float32),
        ),
        grid_spec=pltpu.PrefetchScalarGridSpec(
            num_scalar_prefetch=1,
            grid=(half_f, nr + 1),
            in_specs=[
                pl.BlockSpec((1, rows, depth), lambda fi, t, info: (freq(fi, info), 0, 0)),
                pl.BlockSpec((1, 1, depth, n), col_map),
                pl.BlockSpec((1, 1, depth, n), col_map),
                pl.BlockSpec((2, 1, 1, n, ph), tcol_map),
                pl.BlockSpec(
                    (2, nc, 1, n, ph),
                    lambda fi, t, info: (0, 0, jnp.where(t <= info[0], 0, 1), 0, 0),
                ),
            ],
            out_specs=(
                pl.BlockSpec((2, rows, n), coh_map),
                pl.BlockSpec((half_f, 2, 2, 8, ph), lambda fi, t, info: (0, 0, 0, 0, 0)),
            ),
            scratch_shapes=[
                pltpu.VMEM((3, rows, n), jnp.bfloat16),
                pltpu.VMEM((3, 2, n, ph), jnp.bfloat16),
                pltpu.VMEM((2, 2, rows, ph), jnp.float32),
            ],
        ),
        compiler_params=pltpu.CompilerParams(
            dimension_semantics=("arbitrary", "arbitrary"), vmem_limit_bytes=50 * 2**20
        ),
        name="beam",
    )(info, xrow, xcr, xci, tcol, trow)


def reduce_kernel(ng, nr, nc, stations, part_ref, beam_ref, held, send, recv):
    w, r, c = lax.axis_index("win"), lax.axis_index("srow"), lax.axis_index("scol")
    group, core, tile = w // 2, lax.rem(w, 2), r * nc + c
    tiles = nr * nc

    def place(fi, d, sign):
        to = lax.rem(tile + tiles + sign * d, tiles)
        return lax.rem(group + ng + sign * fi, ng), to

    def where(fi, d, sign):
        g, to = place(fi, d, sign)
        return {"win": 2 * g + core, "srow": to // nc, "scol": lax.rem(to, nc)}

    others = [(fi, d) for d in range(tiles) for fi in range(ng) if (fi, d) != (0, 0)]
    barrier = pltpu.get_barrier_semaphore()
    for fi, d in others:
        pl.semaphore_signal(barrier, inc=1, device_id=where(fi, d, 1), device_id_type=MESH)
    pl.semaphore_wait(barrier, len(others))

    def make(fi, d, dst):
        return pltpu.make_async_remote_copy(
            src_ref=part_ref.at[fi], dst_ref=dst, send_sem=send.at[fi, d], recv_sem=recv.at[fi, d],
            device_id=where(fi, d, 1), device_id_type=MESH,
        )

    sent = [make(fi, d, held.at[group, tile]) for fi, d in others]
    for copy in sent:
        copy.start()
    held[group, tile] = part_ref[0]
    for fi, d in others:
        g, to = place(fi, d, -1)
        make(fi, d, held.at[g, to]).wait_recv()
    beam_ref[...] = jnp.sum(held[...], axis=1) * (1.0 / stations)
    for copy in sent:
        copy.wait_send()


def reduce_beam(part, ng, nr, nc, stations):
    def kernel(*refs):
        reduce_kernel(ng, nr, nc, stations, *refs)

    return pl.pallas_call(
        kernel,
        out_shape=jax.ShapeDtypeStruct((ng,) + part.shape[1:], jnp.float32),
        in_specs=[pl.BlockSpec(memory_space=pltpu.VMEM)],
        out_specs=pl.BlockSpec(memory_space=pltpu.VMEM),
        scratch_shapes=[
            pltpu.VMEM((ng, nr * nc) + part.shape[1:], jnp.float32),
            pltpu.SemaphoreType.DMA((ng, nr * nc)),
            pltpu.SemaphoreType.DMA((ng, nr * nc)),
        ],
        compiler_params=pltpu.CompilerParams(collective_id=1, has_side_effects=True),
        name="reduce_beam",
    )(part)


def body(nw, nr, nc, spectra, bins, travel):
    w, r, c = lax.axis_index("win"), lax.axis_index("srow"), lax.axis_index("scol")
    group, core = w // 2, w % 2
    nf, _, wl, n = spectra.shape
    half_f = nf // 2
    ph = travel.shape[1] // 2
    x = phase_normalized(spectra).reshape(half_f, 2, 2, wl, n).swapaxes(0, 1)
    t = (travel % NFFT).astype(jnp.int16).reshape(n, 2, ph).swapaxes(0, 1)
    xg, tcol, trow = exchange(x, t, nw, nr, nc)
    cols = xg[:, :nr].transpose(2, 1, 3, 0, 4, 5)
    xcr = cols.reshape(half_f, nr, 2 * nw * wl, n)
    xci = jnp.stack([-cols[:, :, 1], cols[:, :, 0]], axis=2).reshape(half_f, nr, 2 * nw * wl, n)
    xrow = xg[:, nr:].transpose(2, 1, 5, 3, 0, 4).reshape(half_f, nc * n, 2 * nw * wl)
    info = jnp.concatenate([
        jnp.stack([r, group]).astype(jnp.int32),
        jnp.stack([bins[(group + i) % half_f * 2 + core] for i in range(half_f)]),
    ])
    coherent, part = beam_call(info, xrow, xcr, xci, tcol, trow, nw * wl)
    part = part.sum(axis=3).swapaxes(1, 2).reshape(half_f, 4 * ph // 128, 128)
    beam = reduce_beam(part, nw // 2, nr, nc, nr * nc * n).reshape(1, 2 * nw * ph)
    return coherent.reshape(1, 2, nc * n, nr, n), beam


def solution(mesh):
    sizes = [mesh.shape[a] for a in ("win", "srow", "scol")]
    placed = (P(None, None, "win", ("srow", "scol")), P(), P(("srow", "scol"), "win"))
    return jax.shard_map(
        functools.partial(body, *sizes),
        mesh=mesh,
        in_specs=placed,
        out_specs=(P("win", None, "srow", None, "scol"), P("win", None)),
        check_vma=False,
    )
```

profile of v0, /device:TPU:0, one launch (start us, length us, event | category | flops | bytes accessed | tf_op | source)
XLA Modules:
  0.0 142.3 jit_solution(7540273260673773577)
XLA Ops:
  0.7 1.4 fusion.2
  2.0 1.4 pad_add_fusion.info
  3.4 1.0 sqrt_bitcast_fusion
  4.4 1.0 divide_convert_fusion
  5.4 0.7 copy.28
  6.1 1.6 %copy.18 = s32[512,512]{0,1:T(8,128)S(1)} copy(s32[512,512]{1,0:T(8,128)} %param.5) | data formatting | bytes 2097152 | tf_op args[2]
  7.6 0.4 fusion.1
  8.0 1.1 copy.21
  9.2 39.7 %exchange.1 = (bf16[4,6,2,2,16,512]{5,4,3,2,1,0:T(8,128)(2,1)}, s16[2,2,4,512,256]{4,3,2,1,0:T(8,128)(2,1)}, s16[2,2,2,512,256]{4,3,2,1,0:T(8,128)(2,1)}) custom-call(bf16[2,2,2,16,512]{4,3,2,1,0:T(8,128)(2,1)} %bitcast.24, s16[2,512,256]{2,1,0:T(8,128)(2,1)} %bitcast.23), custom_call_target="tpu_custom_call" | custom-call | tf_op jit(solution)/shard_map/exchange/pallas_call | solution.py:170
  48.9 1.1 slice_bitcast_fusion.1
  50.0 1.3 slice_bitcast_fusion
  51.3 0.5 copy.22
  51.8 0.4 reshape.30
  52.2 0.3 copy.25.xrow
  52.5 0.1 copy.23
  52.6 0.1 slice_negate_fusion
  52.7 0.1 pad_maximum_fusion
  52.8 0.1 copy.24
  52.9 64.0 %beam.1 = (bf16[2,1024,2048]{2,1,0:T(8,128)(2,1)}, f32[2,2,2,8,256]{4,3,2,1,0:T(8,128)S(1)}) custom-call(s32[4]{0:T(128)S(1)} %pad_add_fusion.info, bf16[2,1024,128]{2,1,0:T(8,128)(2,1)S(1)} %copy.25.xrow, bf16[2,4,128,512]{3,2,1,0:T(8,128)(2,1)S(1)} %bitcast.20, bf16[2,4,128,512]{3,2,1,0:T(8,128)(2,1)S(1)} %bitcast.21, ...), custom_call_target="tpu_custom_call" | custom-call | tf_op jit(solution)/shard_map/beam/pallas_call | solution.py:282
  116.9 14.5 %reshape.33 = bf16[1,2,1024,4,512]{4,3,2,1,0:T(4,128)(2,1)} reshape(bf16[2,1024,2048]{2,1,0:T(8,128)(2,1)} %get-tuple-element.10) | data formatting | bytes 16777216 | tf_op jit(solution)/shard_map/reshape | solution.py:394
  131.4 0.6 reshape.34.refs_0_
  132.0 9.0 %reduce_beam.1 = f32[2,8,128]{2,1,0:T(8,128)} custom-call(f32[2,8,128]{2,1,0:T(8,128)} %reshape.34.refs_0_), custom_call_target="tpu_custom_call" | custom-call | tf_op jit(solution)/shard_map/reduce_beam/pallas_call | solution.py:359
  141.0 1.3 copy.30
  (2 shorter events, 0.0 us)
where the time goes:
time: 143 us; the launch traced here: 142 us
  Pallas kernels  113 us (79%)
  local copies, waits for them, and re-layouts  24.8 us (17%)
  other arithmetic  3.96 us (3%)
    pallas_call x1, Pallas kernels, beam_call(): pl.pallas_call(functools.partial(beam_kernel, nr, nc, total), out_shape=(...  64 us
    pallas_call x1, Pallas kernels, exchange(): pl.pallas_call(functools.partial(exchange_kernel, nw, nr, nc), out_shape=...  39.7 us
    reshape x1, local copies, waits for them, and re-layouts, body(): return (coherent.reshape(1, 2, nc * n, nr, n), beam)  14.5 us
    pallas_call x1, Pallas kernels, reduce_beam(): pl.pallas_call(kernel, out_shape=jax.ShapeDtypeStruct((ng,) + part.shape[...  9.03 us

commit v1 on v0

--- a/solution.py
+++ b/solution.py
@@ -12,7 +12,8 @@
 NFFT = 4096
 MESH = pl.DeviceIdType.MESH
 MAGIC = 12582912.0
-ROWS = 256
+ROWS = 512
+BEAM_ROWS = 1024
 
 
 def phase_normalized(spectra):
@@ -193,21 +194,12 @@
     scale = info[2 + fi].astype(jnp.float32) * (1.0 / NFFT)
     rows = xrow.shape[1]
     n, ph = tcol.shape[3], tcol.shape[4]
-    step = 32
+    step = 64
+    halves = [pl.ds(slab * ph, ph) for slab in range(2)]
 
     @pl.when((fi == 0) & (t == 0))
     def _():
         part[...] = jnp.zeros_like(part)
-
-    for slab in range(2):
-        @pl.loop(0, n // step)
-        def _(i):
-            at = pl.ds(pl.multiple_of(i * step, step), step)
-            cr, ci = steer(tcol[slab, 0, 0, at, :], scale)
-            cr, ci = cr.astype(jnp.bfloat16), ci.astype(jnp.bfloat16)
-            csteer[0, slab, at, :] = cr
-            csteer[1, slab, at, :] = ci
-            csteer[2, slab, at, :] = cr + ci
 
     @pl.when((t == 0) | (t == r + 1))
     def _():
@@ -218,8 +210,35 @@
                     at = pl.ds(pl.multiple_of(i * step, step), step)
                     to = pl.ds(pl.multiple_of(block * n + i * step, step), step)
                     rr, ri = steer(trow[slab, block, 0, at, :], scale)
-                    rsteer[0, slab, to, :] = rr.astype(jnp.bfloat16).astype(jnp.float32)
-                    rsteer[1, slab, to, :] = ri.astype(jnp.bfloat16).astype(jnp.float32)
+                    rsteer[0, to, halves[slab]] = rr.astype(jnp.bfloat16).astype(jnp.float32)
+                    rsteer[1, to, halves[slab]] = ri.astype(jnp.bfloat16).astype(jnp.float32)
+
+    own = (t == r) | (t == r + 1)
+
+    @pl.when(own)
+    def _():
+        @pl.loop(0, n // step)
+        def _(i):
+            at = pl.ds(pl.multiple_of(i * step, step), step)
+            come = pl.ds(pl.multiple_of(info[2 + part.shape[0]] * n + i * step, step), step)
+            cr = rsteer[0, come, :].astype(jnp.bfloat16)
+            ci = rsteer[1, come, :].astype(jnp.bfloat16)
+            csteer[0, at, :] = cr
+            csteer[1, at, :] = ci
+            csteer[2, at, :] = cr + ci
+
+    @pl.when(jnp.logical_not(own))
+    def _():
+        for slab in range(2):
+            @pl.loop(0, n // step)
+            def _(i):
+                at = pl.ds(pl.multiple_of(i * step, step), step)
+                side = halves[slab]
+                cr, ci = steer(tcol[slab, 0, 0, at, :], scale)
+                cr, ci = cr.astype(jnp.bfloat16), ci.astype(jnp.bfloat16)
+                csteer[0, at, side] = cr
+                csteer[1, at, side] = ci
+                csteer[2, at, side] = cr + ci
 
     chunk = min(ROWS, rows)
 
@@ -244,18 +263,20 @@
                 coh[1, at, :] = ki
 
     half = jnp.where(t <= r, 0, 1)
-    weight = jnp.where((t == r) | (t == r + 1), 1.0, 2.0)
+    weight = jnp.where(own, 1.0, 2.0)
+
+    chunk = min(BEAM_ROWS, rows)
 
     @pl.loop(0, rows // chunk)
     def _(m):
         at = pl.ds(pl.multiple_of(m * chunk, chunk), chunk)
-        for slab in range(2):
-            t1 = jnp.dot(kscr[0, at, :], csteer[0, slab], preferred_element_type=jnp.float32)
-            t2 = jnp.dot(kscr[1, at, :], csteer[1, slab], preferred_element_type=jnp.float32)
-            t3 = jnp.dot(kscr[2, at, :], csteer[2, slab], preferred_element_type=jnp.float32)
-            v = rsteer[0, slab, at, :] * (t1 - t2) + rsteer[1, slab, at, :] * (t3 - (t1 + t2))
-            v = jnp.sum(v.reshape(chunk // 8, 8, ph), axis=0)
-            part[fi, half, slab] += weight * v
+        for side in halves:
+            t1 = jnp.dot(kscr[0, at, :], csteer[0, :, side], preferred_element_type=jnp.float32)
+            t2 = jnp.dot(kscr[1, at, :], csteer[1, :, side], preferred_element_type=jnp.float32)
+            t3 = jnp.dot(kscr[2, at, :], csteer[2, :, side], preferred_element_type=jnp.float32)
+            v = rsteer[0, at, side] * (t1 - t2) + rsteer[1, at, side] * (t3 - (t1 + t2))
+            v = jnp.sum(v.reshape(chunk // 8, 8, v.shape[1]), axis=0)
+            part[fi, half, :, side] += weight * v
 
 
 def beam_call(info, xrow, xcr, xci, tcol, trow, total):
@@ -283,7 +304,7 @@
         functools.partial(beam_kernel, nr, nc, total),
         out_shape=(
             jax.ShapeDtypeStruct((2, rows, nr * n), jnp.bfloat16),
-            jax.ShapeDtypeStruct((half_f, 2, 2, 8, ph), jnp.float32),
+            jax.ShapeDtypeStruct((half_f, 2, 8, 2 * ph), jnp.float32),
         ),
         grid_spec=pltpu.PrefetchScalarGridSpec(
             num_scalar_prefetch=1,
@@ -300,12 +321,12 @@
             ],
             out_specs=(
                 pl.BlockSpec((2, rows, n), coh_map),
-                pl.BlockSpec((half_f, 2, 2, 8, ph), lambda fi, t, info: (0, 0, 0, 0, 0)),
+                pl.BlockSpec((half_f, 2, 8, 2 * ph), lambda fi, t, info: (0, 0, 0, 0)),
             ),
             scratch_shapes=[
                 pltpu.VMEM((3, rows, n), jnp.bfloat16),
-                pltpu.VMEM((3, 2, n, ph), jnp.bfloat16),
-                pltpu.VMEM((2, 2, rows, ph), jnp.float32),
+                pltpu.VMEM((3, n, 2 * ph), jnp.bfloat16),
+                pltpu.VMEM((2, rows, 2 * ph), jnp.float32),
             ],
         ),
         compiler_params=pltpu.CompilerParams(
@@ -387,9 +408,10 @@
     info = jnp.concatenate([
         jnp.stack([r, group]).astype(jnp.int32),
         jnp.stack([bins[(group + i) % half_f * 2 + core] for i in range(half_f)]),
+        c[None].astype(jnp.int32),
     ])
     coherent, part = beam_call(info, xrow, xcr, xci, tcol, trow, nw * wl)
-    part = part.sum(axis=3).swapaxes(1, 2).reshape(half_f, 4 * ph // 128, 128)
+    part = part.sum(axis=2).reshape(half_f, 2, 2, ph).swapaxes(1, 2).reshape(half_f, 4 * ph // 128, 128)
     beam = reduce_beam(part, nw // 2, nr, nc, nr * nc * n).reshape(1, 2 * nw * ph)
     return coherent.reshape(1, 2, nc * n, nr, n), beam
 

time: 143 us -> 129 us (0.902)
  Pallas kernels: 113 us -> 98.2 us
    pallas_call x1, Pallas kernels: 64 us -> 49.5 us  [beam_call(): pl.pallas_call(functools.partial(beam_kernel, nr, nc, total), out_shape=(...]
where the time goes in v1:
time: 129 us; the launch traced here: 128 us
  Pallas kernels  98.2 us (76%)
  local copies, waits for them, and re-layouts  26.2 us (20%)
  other arithmetic  2.6 us (2%)
    pallas_call x1, Pallas kernels, beam_call(): pl.pallas_call(functools.partial(beam_kernel, nr, nc, total), out_shape=(...  49.5 us
    pallas_call x1, Pallas kernels, exchange(): pl.pallas_call(functools.partial(exchange_kernel, nw, nr, nc), out_shape=...  39.7 us
    reshape x1, local copies, waits for them, and re-layouts, body(): return (coherent.reshape(1, 2, nc * n, nr, n), beam)  14.5 us
    pallas_call x1, Pallas kernels, reduce_beam(): pl.pallas_call(kernel, out_shape=jax.ShapeDtypeStruct((ng,) + part.shape[...  9.01 us
    unnamed x2, local copies, waits for them, and re-layouts  2.85 us

profile of v1, /device:TPU:0, one launch (start us, length us, event | category | flops | bytes accessed | tf_op | source)
XLA Modules:
  0.0 127.8 jit_solution(4567526840323668804)
XLA Ops:
  0.7 1.4 %fusion.2 = (s32[1]{0:T(128)}, s32[1]{0:T(128)}) fusion(s32[4]{0:T(128)} %param.4, s32[]{:T(128)S(6)} %select_n.36, s32[]{:T(128)S(6)} %select_n.34), kind=kLoop, calls=%fused_computation.12 | loop fusion | bytes 24 | tf_op jit(solution)/shard_map/dynamic_slice | solution.py:410
  2.1 1.3 %concatenate.3.info = s32[5]{0:T(128)S(1)} concatenate(s32[1]{0:T(128)} %bitcast, s32[1]{0:T(128)} %bitcast.1, s32[1]{0:T(128)} %get-tuple-element.15, s32[1]{0:T(128)} %get-tuple-element.14, s32[1]{0:T(128)} %bitcast.2), dimensions={0} | concatenate | bytes 40 | tf_op jit(solution)/shard_map/concatenate | solution.py:408
  3.4 1.0 sqrt_bitcast_fusion
  4.5 1.0 divide_convert_fusion
  5.4 0.7 copy.18
  6.1 1.6 %copy.9 = s32[512,512]{0,1:T(8,128)S(1)} copy(s32[512,512]{1,0:T(8,128)} %param.5) | data formatting | bytes 2097152 | tf_op args[2]
  7.7 0.4 fusion.1
  8.1 1.1 copy.12
  9.2 39.7 %exchange.1 = (bf16[4,6,2,2,16,512]{5,4,3,2,1,0:T(8,128)(2,1)}, s16[2,2,4,512,256]{4,3,2,1,0:T(8,128)(2,1)}, s16[2,2,2,512,256]{4,3,2,1,0:T(8,128)(2,1)}) custom-call(bf16[2,2,2,16,512]{4,3,2,1,0:T(8,128)(2,1)} %bitcast.27, s16[2,512,256]{2,1,0:T(8,128)(2,1)} %bitcast.26), custom_call_target="tpu_custom_call" | custom-call | tf_op jit(solution)/shard_map/exchange/pallas_call | solution.py:171
  48.9 1.1 slice_bitcast_fusion.1
  50.0 1.3 %slice_bitcast_fusion = bf16[2,4,2,4,16,512]{5,4,2,0,1,3:T(8,128)(2,1)S(1)} fusion(bf16[4,6,2,2,16,512]{5,4,3,2,1,0:T(8,128)(2,1)} %get-tuple-element.7), kind=kLoop, calls=%fused_computation.6 | loop fusion | bytes 2097152 | tf_op jit(solution)/shard_map/transpose | solution.py:404
  51.3 0.5 copy.13
  51.9 0.4 reshape.33
  52.2 0.3 copy.16.xrow
  52.5 0.1 copy.14
  52.6 0.1 slice_negate_fusion
  52.7 0.1 pad_maximum_fusion
  52.8 0.1 copy.15
  52.9 49.5 %beam.1 = (bf16[2,1024,2048]{2,1,0:T(8,128)(2,1)}, f32[2,2,8,512]{3,2,1,0:T(8,128)S(1)}) custom-call(s32[5]{0:T(128)S(1)} %concatenate.3.info, bf16[2,1024,128]{2,1,0:T(8,128)(2,1)S(1)} %copy.16.xrow, bf16[2,4,128,512]{3,2,1,0:T(8,128)(2,1)S(1)} %bitcast.23, bf16[2,4,128,512]{3,2,1,0:T(8,128)(2,1)S(1)} %bitcast.24, ...), custom_call_target="tpu_custom_call" | custom-call | tf_op jit(solution)/shard_map/beam/pallas_call | solution.py:303
  102.4 14.5 %reshape.36 = bf16[1,2,1024,4,512]{4,3,2,1,0:T(4,128)(2,1)} reshape(bf16[2,1024,2048]{2,1,0:T(8,128)(2,1)} %get-tuple-element.10) | data formatting | bytes 16777216 | tf_op jit(solution)/shard_map/reshape | solution.py:416
  116.9 0.6 reshape.38.refs_0_
  117.5 9.0 %reduce_beam.1 = f32[2,8,128]{2,1,0:T(8,128)} custom-call(f32[2,8,128]{2,1,0:T(8,128)} %reshape.38.refs_0_), custom_call_target="tpu_custom_call" | custom-call | tf_op jit(solution)/shard_map/reduce_beam/pallas_call | solution.py:380
  126.5 1.3 %copy.20 = f32[1,2048]{1,0:T(1,128)} copy(f32[1,2048]{1,0:T(1,128)} %bitcast.30) | data formatting | bytes 16384
  (1 shorter events, 0.0 us)
